TPU v7x, 256 devices: a whole 4x4x8 slice. The times are simulated.
256 devices in a mesh: seq: 64 (over z, y, core), tp: 4 (over x).
Axes of the slice: x: 4, y: 4, z: 8, core: 2. Of those that a mesh axis runs over, the one named last changes fastest.
Arguments:
- text_query_matrix: bfloat16 [16384, 8192], P('seq', 'tp'), may hold values from -12 to 12
- vision: bfloat16 [16384, 8192], P(('seq', 'tp')), may hold values from -12 to 12
- key_matrix: bfloat16 [8192, 1024], P(None, 'tp'), may hold values from -0.0625 to 0.0625
- value_matrix: bfloat16 [8192, 1024], P(None, 'tp'), may hold values from -0.0625 to 0.0625
- query_norm_gain: float32 [128], replicated, may hold values from 0.5 to 1.5
- key_gain: float32 [128], replicated, may hold values from 0.5 to 1.5
- block_mask: int32 [256, 64], P('seq'), may hold values from 0 to 1, as said below
Outputs:
- attended: bfloat16 [16384, 8192], P('seq', 'tp')
Inputs may be any that keep to these rules, and one draw needn't show every extreme that they name: block_mask[b, i] is 1 on exactly one run of consecutive blocks b; the run starts in the blocks of text shard i (blocks i * 4 to (i + 1) * 4 - 1) and ends at or before the last block of text shard i + 3; in every draw some image's run ends exactly at that last block.
All inputs are finite; a program needn't handle non-finite values.
Results may differ from a plain program's by a relative error of at most 0.0076.
Values may be sent and summed in bfloat16 or wider, within the bound.
No kernel may reach another device: no remote copies, remote signals or barrier semaphores. Data moves between devices by JAX's collectives and lax.ppermute only.
A program may use at most 128 MiB of HBM per device.

v0:
```python
import jax
import jax.numpy as jnp
from jax import lax
from jax.sharding import PartitionSpec as P

HEAD_SIZE = 128
REACH = 4
BLOCK = 64


def shifted(value, axis, by):
    length = lax.axis_size(axis)
    pairs = [(i, i + by) for i in range(length) if 0 <= i + by < length]
    return lax.ppermute(value, axis, pairs)


def heads_normalized(tensor, scale_gain):
    return (
        tensor * lax.rsqrt(jnp.mean(tensor * tensor, axis=-1, keepdims=True) + 1e-05) * scale_gain
    )


def project(vision_rows, key_matrix, value_matrix, key_gain):
    kv_heads = key_matrix.shape[1] // HEAD_SIZE
    count = vision_rows.shape[0]
    key_projected = jnp.dot(vision_rows, key_matrix, preferred_element_type=jnp.float32).reshape(
        count, kv_heads, HEAD_SIZE
    )
    key_matrix_rows = (
        heads_normalized(key_projected, key_gain)
        .astype(jnp.bfloat16)
        .reshape(count, kv_heads * HEAD_SIZE)
    )
    value_matrix_rows = jnp.dot(
        vision_rows, value_matrix, preferred_element_type=jnp.float32
    ).astype(jnp.bfloat16)
    return jnp.stack([key_matrix_rows, value_matrix_rows])


def attend(carried, kv_block, weight_col, queries):
    totals, accumulated = carried
    kv_heads = queries.shape[1]
    score_scale = HEAD_SIZE ** (-0.5)
    split_block = kv_block.reshape(2, kv_block.shape[1], kv_heads, HEAD_SIZE)
    new_totals = []
    new_sums = []
    for kv_index in range(kv_heads):
        scores = (
            jnp.einsum(
                "tgd,kd->gtk",
                queries[:, kv_index],
                split_block[0, :, kv_index],
                preferred_element_type=jnp.float32,
            )
            * score_scale
        )
        weights = jnp.exp(scores) * weight_col[None, :, None]
        new_totals.append(totals[kv_index] + jnp.sum(weights, axis=2))
        new_sums.append(
            accumulated[:, kv_index]
            + jnp.einsum(
                "gtk,kd->tgd",
                weights.astype(jnp.bfloat16),
                split_block[1, :, kv_index],
                preferred_element_type=jnp.float32,
            )
        )
    return (jnp.stack(new_totals), jnp.stack(new_sums, axis=1))


def body(
    text_query_matrix, vision, key_matrix, value_matrix, query_norm_gain, key_gain, block_mask
):
    vision_rows = lax.all_gather(vision, "tp", axis=0, tiled=True)
    kv_heads = key_matrix.shape[1] // HEAD_SIZE
    query_group_width = text_query_matrix.shape[1] // HEAD_SIZE // kv_heads
    text_rows = text_query_matrix.shape[0]
    queries = heads_normalized(
        text_query_matrix.astype(jnp.float32).reshape(
            text_rows, kv_heads, query_group_width, HEAD_SIZE
        ),
        query_norm_gain,
    ).astype(jnp.bfloat16)
    arrivals = [vision_rows] + [
        shifted(vision_rows, "seq", distance) for distance in range(1, REACH)
    ]
    kv_blocks = [project(arrived, key_matrix, value_matrix, key_gain) for arrived in arrivals]
    carried = (
        jnp.zeros((kv_heads, query_group_width, text_rows), jnp.float32),
        jnp.zeros((text_rows, kv_heads, query_group_width, HEAD_SIZE), jnp.float32),
    )
    position = lax.axis_index("seq")
    for distance in range(REACH):
        image_index = position - distance
        column = lax.dynamic_slice_in_dim(block_mask, jnp.maximum(image_index, 0), 1, 1)[:, 0]
        column = jnp.where(image_index >= 0, column, jnp.zeros_like(column))
        weight_col = jnp.repeat(column.astype(jnp.float32), BLOCK)
        carried = attend(carried, kv_blocks[distance], weight_col, queries)
    totals, accumulated = carried
    totals_t = jnp.transpose(totals, (2, 0, 1))[..., None]
    has_image = totals_t > 0
    averaged = accumulated / jnp.where(has_image, totals_t, jnp.ones_like(totals_t))
    result_rows = jnp.where(has_image, averaged, jnp.zeros_like(averaged))
    return result_rows.astype(jnp.bfloat16).reshape(
        text_rows, kv_heads * query_group_width * HEAD_SIZE
    )


def solution(mesh):
    placed = (
        P("seq", "tp"),
        P(("seq", "tp"), None),
        P(None, "tp"),
        P(None, "tp"),
        P(),
        P(),
        P("seq", None),
    )
    return jax.shard_map(
        body, mesh=mesh, in_specs=placed, out_specs=P("seq", "tp"), check_vma=False
    )
```

profile of v0, /device:TPU:32, one launch (start us, length us, event | category | flops | bytes accessed | tf_op | source)
XLA Modules:
  0.0 340.6 jit_solution(10686656299928051354)
XLA Ops:
  7.3 55.3 %all-gather.2.cloned.1.call-done = bf16[256,8192]{1,0:T(8,128)(2,1)} async-done(((bf16[64,8192]{1,0:T(8,128)(2,1)}), bf16[256,8192]{1,0:T(8,128)(2,1)}) %all-gather.2.cloned.1.call-update) | async-done | bytes 4194320 | tf_op jit(solution)/shard_map/all_gather | solution.py:74
  62.6 2.8 collective-permute-start.2
  65.4 3.4 collective-permute-start.1
  68.8 2.9 collective-permute-start
  71.8 1.1 convert_reduce_fusion
  73.5 1.5 copy.19
  76.5 1.2 copy-done
  77.7 4.0 %bitcast_reduce_fusion.11 = (f32[256,2]{0,1:T(2,128)S(1)}, f32[256,256]{0,1:T(8,128)S(1)}) fusion(bf16[256,8192]{1,0:T(8,128)(2,1)} %all-gather.2.cloned.1.call-done, bf16[8192,256]{1,0:T(8,128)(2,1)S(1)} %copy-done), kind=kOutput, calls=%fused_computation.72 | convolution fusion | flops 1073872384 | bytes 8652800 | tf_op jit(solution)/shard_map/dot_general | solution.py:26
  81.9 5.3 %convolution_convert_fusion.3 = bf16[256,256]{0,1:T(8,128)(2,1)S(1)} fusion(bf16[256,8192]{1,0:T(8,128)(2,1)} %all-gather.2.cloned.1.call-done, bf16[8192,256]{1,0:T(8,128)(2,1)} %param.10), kind=kOutput, calls=%fused_computation.40 | convolution fusion | flops 1073807360 | bytes 8519680 | tf_op jit(solution)/shard_map/dot_general | solution.py:34
  87.2 67.9 %collective-permute-done.2 = bf16[256,8192]{1,0:T(8,128)(2,1)} collective-permute-done((bf16[256,8192]{1,0:T(8,128)(2,1)}, bf16[256,8192]{1,0:T(8,128)(2,1)}, u32[]{:S(2)}, u32[]{:S(2)}) %collective-permute-start.2) | collective-permute-done | bytes 4194336 | tf_op jit(solution)/shard_map/ppermute | solution.py:14
  155.1 4.0 %bitcast_reduce_fusion.8 = (f32[256,2]{0,1:T(2,128)S(1)}, f32[256,256]{0,1:T(8,128)S(1)}) fusion(bf16[256,8192]{1,0:T(8,128)(2,1)} %collective-permute-done.2, bf16[8192,256]{1,0:T(8,128)(2,1)S(1)} %copy-done.1), kind=kOutput, calls=%fused_computation.69 | convolution fusion | flops 1073872384 | bytes 8652800 | tf_op jit(solution)/shard_map/dot_general | solution.py:26
  159.3 97.8 %collective-permute-done.1 = bf16[256,8192]{1,0:T(8,128)(2,1)} collective-permute-done((bf16[256,8192]{1,0:T(8,128)(2,1)}, bf16[256,8192]{1,0:T(8,128)(2,1)}, u32[]{:S(2)}, u32[]{:S(2)}) %collective-permute-start.1) | collective-permute-done | bytes 4194336 | tf_op jit(solution)/shard_map/ppermute | solution.py:14
  257.1 5.2 %bitcast_reduce_fusion.9 = (f32[256,2]{0,1:T(2,128)S(1)}, f32[256,256]{0,1:T(8,128)S(1)}) fusion(bf16[256,8192]{1,0:T(8,128)(2,1)} %collective-permute-done.1, bf16[8192,256]{1,0:T(8,128)(2,1)} %param.9), kind=kOutput, calls=%fused_computation.70 | convolution fusion | flops 1073872384 | bytes 8652800 | tf_op jit(solution)/shard_map/dot_general | solution.py:26
  262.5 40.5 %collective-permute-done = bf16[256,8192]{1,0:T(8,128)(2,1)} collective-permute-done((bf16[256,8192]{1,0:T(8,128)(2,1)}, bf16[256,8192]{1,0:T(8,128)(2,1)}, u32[]{:S(2)}, u32[]{:S(2)}) %collective-permute-start) | collective-permute-done | bytes 4194336 | tf_op jit(solution)/shard_map/ppermute | solution.py:14
  302.9 5.2 %bitcast_reduce_fusion.10 = (f32[256,2]{0,1:T(2,128)S(1)}, f32[256,256]{0,1:T(8,128)S(1)}) fusion(bf16[256,8192]{1,0:T(8,128)(2,1)} %collective-permute-done, bf16[8192,256]{1,0:T(8,128)(2,1)} %param.9), kind=kOutput, calls=%fused_computation.71 | convolution fusion | flops 1073872384 | bytes 8652800 | tf_op jit(solution)/shard_map/dot_general | solution.py:26
  310.4 0.9 bitcast_reduce_fusion.4
  311.3 1.1 bitcast_reduce_fusion.6
  312.4 0.9 bitcast_reduce_fusion.5
  313.4 0.9 bitcast_reduce_fusion.7
  315.4 1.1 copy-done.2
  316.5 4.0 %convolution_convert_fusion.2 = bf16[256,256]{0,1:T(8,128)(2,1)S(1)} fusion(bf16[256,8192]{1,0:T(8,128)(2,1)} %collective-permute-done, bf16[8192,256]{1,0:T(8,128)(2,1)S(1)} %copy-done.2), kind=kOutput, calls=%fused_computation.39 | convolution fusion | flops 1073807360 | bytes 8519680 | tf_op jit(solution)/shard_map/dot_general | solution.py:34
  321.1 4.0 %convolution_convert_fusion.1 = bf16[256,256]{0,1:T(8,128)(2,1)S(1)} fusion(bf16[256,8192]{1,0:T(8,128)(2,1)} %collective-permute-done.1, bf16[8192,256]{1,0:T(8,128)(2,1)S(1)} %copy-done.2), kind=kOutput, calls=%fused_computation.38 | convolution fusion | flops 1073807360 | bytes 8519680 | tf_op jit(solution)/shard_map/dot_general | solution.py:34
  325.7 4.0 %convolution_convert_fusion = bf16[256,256]{0,1:T(8,128)(2,1)S(1)} fusion(bf16[256,8192]{1,0:T(8,128)(2,1)} %collective-permute-done.2, bf16[8192,256]{1,0:T(8,128)(2,1)S(1)} %copy-done.2), kind=kOutput, calls=%fused_computation.37 | convolution fusion | flops 1073807360 | bytes 8519680 | tf_op jit(solution)/shard_map/dot_general | solution.py:34
  332.4 1.4 copy.32
  (46 shorter events, 10.2 us)
Async XLA Ops:
  6.5 56.1 %all-gather.2.cloned.1.call-start = ((), (), s32[]{:S(2)}) async-start(), calls=%async_computation | async-start | bytes 5242880 | tf_op jit(solution)/shard_map/all_gather | solution.py:74
  62.6 92.5 %collective-permute-start.2 = (bf16[256,8192]{1,0:T(8,128)(2,1)}, bf16[256,8192]{1,0:T(8,128)(2,1)}, u32[]{:S(2)}, u32[]{:S(2)}) collective-permute-start(bf16[256,8192]{1,0:T(8,128)(2,1)} %all-gather.2.cloned.1.call-done), channel_id=1, source_target_pairs={{0,12},{4,16},{8,20},{12,24},{16,28},{20,32},{24,36},{28,40},{32,4... | collective-permute-start | bytes 12582920 | tf_op jit(solution)/shard_map/ppermute | solution.py:14
  65.4 191.7 %collective-permute-start.1 = (bf16[256,8192]{1,0:T(8,128)(2,1)}, bf16[256,8192]{1,0:T(8,128)(2,1)}, u32[]{:S(2)}, u32[]{:S(2)}) collective-permute-start(bf16[256,8192]{1,0:T(8,128)(2,1)} %all-gather.2.cloned.1.call-done), channel_id=1, source_target_pairs={{0,8},{4,12},{8,16},{12,20},{16,24},{20,28},{24,32},{28,36},{32,40... | collective-permute-start | bytes 12582920 | tf_op jit(solution)/shard_map/ppermute | solution.py:14
  68.8 234.1 %collective-permute-start = (bf16[256,8192]{1,0:T(8,128)(2,1)}, bf16[256,8192]{1,0:T(8,128)(2,1)}, u32[]{:S(2)}, u32[]{:S(2)}) collective-permute-start(bf16[256,8192]{1,0:T(8,128)(2,1)} %all-gather.2.cloned.1.call-done), channel_id=1, source_target_pairs={{0,4},{4,8},{8,12},{12,16},{16,20},{20,24},{24,28},{28,32},{32,36}... | collective-permute-start | bytes 12582920 | tf_op jit(solution)/shard_map/ppermute | solution.py:14
  75.0 0.8 copy-start.4
  75.5 2.2 copy-start
  81.9 73.2 %copy-start.1 = (bf16[8192,256]{1,0:T(8,128)(2,1)S(1)}, bf16[8192,256]{1,0:T(8,128)(2,1)}, u32[]{:S(2)}) copy-start(bf16[8192,256]{1,0:T(8,128)(2,1)} %param.9) | copy-start | bytes 12582916
  262.4 45.9 %copy-start.3 = (f32[128]{0:T(128)S(1)}, f32[128]{0:T(128)}, u32[]{:S(2)}) copy-start(f32[128]{0:T(128)} %param.12) | copy-start | bytes 1540
  314.3 2.2 copy-start.2
Sparse Core Ops, SparseCore 0:
  9.2 53.3 all-gather.1
where the time goes:
time: 341 us
  waiting for transfers between devices  262 us (77%)
  matrix products  46 us (13%)
  between operations  13.7 us (4%)
  starting transfers between devices  9.15 us (3%)
  local copies, waits for them, and re-layouts  6.85 us (2%)
    ppermute x3, waiting for transfers between devices, shifted(): return lax.ppermute(value, axis, pairs)  206 us
    all_gather x1, waiting for transfers between devices, body(): vision_rows = lax.all_gather(vision, 'tp', axis=0, tiled=True)  55.3 us
    dot_general x4, matrix products, project(): jnp.dot(vision_rows, key_matrix, preferred_element_type=jnp.float32)  18.5 us
    dot_general x4, matrix products, project(): jnp.dot(vision_rows, value_matrix, preferred_element_type=jnp.float32)  17.4 us
    ppermute x3, starting transfers between devices, shifted(): return lax.ppermute(value, axis, pairs)  9.15 us
  transfers between devices with their start and end apart: 4, of which 4 were waited for; matrix products, arithmetic and copies ran while one was open for 7% of the time, Pallas kernels for 0%

commit v1 on v0

--- a/solution.py
+++ b/solution.py
@@ -6,6 +6,22 @@
 HEAD_SIZE = 128
 REACH = 4
 BLOCK = 64
+
+
+def collect(x, axis, dim):
+    ways, here, step = (lax.axis_size(axis), lax.axis_index(axis), x.shape[dim])
+    lengths = [n * ways if d == dim else n for d, n in enumerate(x.shape)]
+    full = lax.dynamic_update_slice_in_dim(jnp.zeros(lengths, x.dtype), x, here * step, axis=dim)
+    going_up = going_down = x
+    for far in range(1, ways // 2 + 1):
+        going_up = lax.ppermute(going_up, axis, [(d, (d + 1) % ways) for d in range(ways)])
+        full = lax.dynamic_update_slice_in_dim(full, going_up, (here - far) % ways * step, axis=dim)
+        if 2 * far < ways:
+            going_down = lax.ppermute(going_down, axis, [(d, (d - 1) % ways) for d in range(ways)])
+            full = lax.dynamic_update_slice_in_dim(
+                full, going_down, (here + far) % ways * step, axis=dim
+            )
+    return full
 
 
 def shifted(value, axis, by):
@@ -71,7 +87,7 @@
 def body(
     text_query_matrix, vision, key_matrix, value_matrix, query_norm_gain, key_gain, block_mask
 ):
-    vision_rows = lax.all_gather(vision, "tp", axis=0, tiled=True)
+    vision_rows = collect(vision, "tp", 0)
     kv_heads = key_matrix.shape[1] // HEAD_SIZE
     query_group_width = text_query_matrix.shape[1] // HEAD_SIZE // kv_heads
     text_rows = text_query_matrix.shape[0]

time: 341 us -> 324 us (0.950)
  between operations: 13.7 us -> 0.36 us
  waiting for transfers between devices: 262 us -> 249 us
  local copies, waits for them, and re-layouts: 6.85 us -> 12.4 us
  starting transfers between devices: 9.15 us -> 12.9 us
    all_gather x1 -> x0, waiting for transfers between devices: 55.3 us -> none  [body(): vision_rows = lax.all_gather(vision, 'tp', axis=0, tiled=True)]
    ppermute x0 -> x3, waiting for transfers between devices: none -> 42.4 us  [the longest x2 42.4 us: collect(): lax.ppermute(going_up, axis, [(d, (d + 1) % ways) for d in range(ways)])]
    dynamic_update_slice x0 -> x4, local copies, waits for them, and re-layouts: none -> 4.26 us  [the longest x2 2.08 us: collect(): lax.dynamic_update_slice_in_dim(full, going_up, (here - far) % ways * ste...]
    ppermute x0 -> x3, starting transfers between devices: none -> 3.52 us  [the longest x2 1.77 us: collect(): lax.ppermute(going_up, axis, [(d, (d + 1) % ways) for d in range(ways)])]
  transfers between devices with their start and end apart: 4 -> 6, of which waited for: 4 -> 5; matrix products, arithmetic and copies ran while one was open for 7% -> 9% of each run, Pallas kernels for 0% -> 0%
where the time goes in v1:
time: 324 us; the launch traced here: 323 us
  waiting for transfers between devices  249 us (77%)
  matrix products  46 us (14%)
  starting transfers between devices  12.9 us (4%)
  local copies, waits for them, and re-layouts  12.4 us (4%)
    ppermute x3, waiting for transfers between devices, shifted(): return lax.ppermute(value, axis, pairs)  207 us
    ppermute x2, waiting for transfers between devices, collect(): lax.ppermute(going_up, axis, [(d, (d + 1) % ways) for d in range(ways)])  42.4 us
    dot_general x4, matrix products, project(): jnp.dot(vision_rows, key_matrix, preferred_element_type=jnp.float32)  18.5 us
    dot_general x4, matrix products, project(): jnp.dot(vision_rows, value_matrix, preferred_element_type=jnp.float32)  17.4 us
    ppermute x3, starting transfers between devices, shifted(): return lax.ppermute(value, axis, pairs)  9.42 us
  transfers between devices with their start and end apart: 6, of which 5 were waited for; matrix products, arithmetic and copies ran while one was open for 9% of the time, Pallas kernels for 0%

profile of v1, /device:TPU:32, one launch (start us, length us, event | category | flops | bytes accessed | tf_op | source)
XLA Modules:
  0.0 322.8 jit_solution(11250094145926816063)
XLA Ops:
  0.0 1.5 collective-permute-start
  1.5 1.7 collective-permute-start.1
  3.2 2.4 broadcast_in_dim.19
  5.7 1.1 constant_dynamic-update-slice_fusion.3
  6.8 19.5 %collective-permute-done = bf16[64,8192]{1,0:T(8,128)(2,1)S(1)} collective-permute-done((bf16[64,8192]{1,0:T(8,128)(2,1)}, bf16[64,8192]{1,0:T(8,128)(2,1)S(1)}, u32[]{:S(2)}, u32[]{:S(2)}) %collective-permute-start) | collective-permute-done | bytes 1048608 | tf_op jit(solution)/shard_map/ppermute | solution.py:17
  28.7 22.9 %collective-permute-done.2 = bf16[64,8192]{1,0:T(8,128)(2,1)S(1)} collective-permute-done((bf16[64,8192]{1,0:T(8,128)(2,1)S(1)}, bf16[64,8192]{1,0:T(8,128)(2,1)S(1)}, u32[]{:S(2)}, u32[]{:S(2)}) %collective-permute-start.2) | collective-permute-done | bytes 1048608 | tf_op jit(solution)/shard_map/ppermute | solution.py:17
  51.6 1.0 constant_dynamic-update-slice_fusion
  52.6 1.9 collective-permute-start.5
  54.5 3.5 %collective-permute-start.4 = (bf16[256,8192]{1,0:T(8,128)(2,1)}, bf16[256,8192]{1,0:T(8,128)(2,1)}, u32[]{:S(2)}, u32[]{:S(2)}) collective-permute-start(bf16[256,8192]{1,0:T(8,128)(2,1)} %constant_dynamic-update-slice_fusion), channel_id=1, source_target_pairs={{0,8},{4,12},{8,16},{12,20},{16,24},{20,28},{24,32},{28,36},{32,40... | collective-permute-start | bytes 12582920 | tf_op jit(solution)/shard_map/ppermute | solution.py:30
  58.0 4.0 %collective-permute-start.3 = (bf16[256,8192]{1,0:T(8,128)(2,1)}, bf16[256,8192]{1,0:T(8,128)(2,1)}, u32[]{:S(2)}, u32[]{:S(2)}) collective-permute-start(bf16[256,8192]{1,0:T(8,128)(2,1)} %constant_dynamic-update-slice_fusion), channel_id=1, source_target_pairs={{0,4},{4,8},{8,12},{12,16},{16,20},{20,24},{24,28},{28,32},{32,36}... | collective-permute-start | bytes 12582920 | tf_op jit(solution)/shard_map/ppermute | solution.py:30
  66.2 4.0 %bitcast_reduce_fusion.11 = (f32[256,2]{0,1:T(2,128)S(1)}, f32[256,256]{0,1:T(8,128)S(1)}) fusion(bf16[256,8192]{1,0:T(8,128)(2,1)} %constant_dynamic-update-slice_fusion, bf16[8192,256]{1,0:T(8,128)(2,1)S(1)} %copy-done), kind=kOutput, calls=%fused_computation.72 | convolution fusion | flops 1073872384 | bytes 8652800 | tf_op jit(solution)/shard_map/dot_general | solution.py:42
  70.4 5.3 %convolution_convert_fusion.3 = bf16[256,256]{0,1:T(8,128)(2,1)S(1)} fusion(bf16[256,8192]{1,0:T(8,128)(2,1)} %constant_dynamic-update-slice_fusion, bf16[8192,256]{1,0:T(8,128)(2,1)} %param.10), kind=kOutput, calls=%fused_computation.40 | convolution fusion | flops 1073807360 | bytes 8519680 | tf_op jit(solution)/shard_map/dot_general | solution.py:50
  75.7 67.4 %collective-permute-done.5 = bf16[256,8192]{1,0:T(8,128)(2,1)} collective-permute-done((bf16[256,8192]{1,0:T(8,128)(2,1)}, bf16[256,8192]{1,0:T(8,128)(2,1)}, u32[]{:S(2)}, u32[]{:S(2)}) %collective-permute-start.5) | collective-permute-done | bytes 4194336 | tf_op jit(solution)/shard_map/ppermute | solution.py:30
  143.1 4.0 %bitcast_reduce_fusion.8 = (f32[256,2]{0,1:T(2,128)S(1)}, f32[256,256]{0,1:T(8,128)S(1)}) fusion(bf16[256,8192]{1,0:T(8,128)(2,1)} %collective-permute-done.5, bf16[8192,256]{1,0:T(8,128)(2,1)S(1)} %copy-done.1), kind=kOutput, calls=%fused_computation.69 | convolution fusion | flops 1073872384 | bytes 8652800 | tf_op jit(solution)/shard_map/dot_general | solution.py:42
  147.3 97.6 %collective-permute-done.4 = bf16[256,8192]{1,0:T(8,128)(2,1)} collective-permute-done((bf16[256,8192]{1,0:T(8,128)(2,1)}, bf16[256,8192]{1,0:T(8,128)(2,1)}, u32[]{:S(2)}, u32[]{:S(2)}) %collective-permute-start.4) | collective-permute-done | bytes 4194336 | tf_op jit(solution)/shard_map/ppermute | solution.py:30
  244.9 5.2 %bitcast_reduce_fusion.9 = (f32[256,2]{0,1:T(2,128)S(1)}, f32[256,256]{0,1:T(8,128)S(1)}) fusion(bf16[256,8192]{1,0:T(8,128)(2,1)} %collective-permute-done.4, bf16[8192,256]{1,0:T(8,128)(2,1)} %param.9), kind=kOutput, calls=%fused_computation.70 | convolution fusion | flops 1073872384 | bytes 8652800 | tf_op jit(solution)/shard_map/dot_general | solution.py:42
  250.3 41.6 %collective-permute-done.3 = bf16[256,8192]{1,0:T(8,128)(2,1)} collective-permute-done((bf16[256,8192]{1,0:T(8,128)(2,1)}, bf16[256,8192]{1,0:T(8,128)(2,1)}, u32[]{:S(2)}, u32[]{:S(2)}) %collective-permute-start.3) | collective-permute-done | bytes 4194336 | tf_op jit(solution)/shard_map/ppermute | solution.py:30
  291.9 5.2 %bitcast_reduce_fusion.10 = (f32[256,2]{0,1:T(2,128)S(1)}, f32[256,256]{0,1:T(8,128)S(1)}) fusion(bf16[256,8192]{1,0:T(8,128)(2,1)} %collective-permute-done.3, bf16[8192,256]{1,0:T(8,128)(2,1)} %param.9), kind=kOutput, calls=%fused_computation.71 | convolution fusion | flops 1073872384 | bytes 8652800 | tf_op jit(solution)/shard_map/dot_general | solution.py:42
  300.3 1.1 bitcast_reduce_fusion.6
  304.5 1.1 copy-done.2
  305.6 4.0 %convolution_convert_fusion.2 = bf16[256,256]{0,1:T(8,128)(2,1)S(1)} fusion(bf16[256,8192]{1,0:T(8,128)(2,1)} %collective-permute-done.3, bf16[8192,256]{1,0:T(8,128)(2,1)S(1)} %copy-done.2), kind=kOutput, calls=%fused_computation.39 | convolution fusion | flops 1073807360 | bytes 8519680 | tf_op jit(solution)/shard_map/dot_general | solution.py:50
  310.2 4.0 %convolution_convert_fusion.1 = bf16[256,256]{0,1:T(8,128)(2,1)S(1)} fusion(bf16[256,8192]{1,0:T(8,128)(2,1)} %collective-permute-done.4, bf16[8192,256]{1,0:T(8,128)(2,1)S(1)} %copy-done.2), kind=kOutput, calls=%fused_computation.38 | convolution fusion | flops 1073807360 | bytes 8519680 | tf_op jit(solution)/shard_map/dot_general | solution.py:50
  314.8 4.0 %convolution_convert_fusion = bf16[256,256]{0,1:T(8,128)(2,1)S(1)} fusion(bf16[256,8192]{1,0:T(8,128)(2,1)} %collective-permute-done.5, bf16[8192,256]{1,0:T(8,128)(2,1)S(1)} %copy-done.2), kind=kOutput, calls=%fused_computation.37 | convolution fusion | flops 1073807360 | bytes 8519680 | tf_op jit(solution)/shard_map/dot_general | solution.py:50
  321.4 1.4 copy.32
  (60 shorter events, 16.6 us)
Async XLA Ops:
  0.0 26.3 %collective-permute-start = (bf16[64,8192]{1,0:T(8,128)(2,1)}, bf16[64,8192]{1,0:T(8,128)(2,1)S(1)}, u32[]{:S(2)}, u32[]{:S(2)}) collective-permute-start(bf16[64,8192]{1,0:T(8,128)(2,1)} %param.8), channel_id=1, source_target_pairs={{0,1},{1,2},{2,3},{3,0},{4,5},{5,6},{6,7},{7,4},{8,9},{9,10},{10,1... | collective-permute-start | bytes 3145736 | tf_op jit(solution)/shard_map/ppermute | solution.py:17
  1.5 26.2 %collective-permute-start.1 = (bf16[64,8192]{1,0:T(8,128)(2,1)}, bf16[64,8192]{1,0:T(8,128)(2,1)S(1)}, u32[]{:S(2)}, u32[]{:S(2)}) collective-permute-start(bf16[64,8192]{1,0:T(8,128)(2,1)} %param.8), channel_id=1, source_target_pairs={{0,3},{1,0},{2,1},{3,2},{4,7},{5,4},{6,5},{7,6},{8,11},{9,8},{10,9... | collective-permute-start | bytes 3145736 | tf_op jit(solution)/shard_map/ppermute | solution.py:20
  3.2 2.5 copy-start.3
  26.3 25.2 %collective-permute-start.2 = (bf16[64,8192]{1,0:T(8,128)(2,1)S(1)}, bf16[64,8192]{1,0:T(8,128)(2,1)S(1)}, u32[]{:S(2)}, u32[]{:S(2)}) collective-permute-start(bf16[64,8192]{1,0:T(8,128)(2,1)S(1)} %collective-permute-done), channel_id=1, source_target_pairs={{0,1},{1,2},{2,3},{3,0},{4,5},{5,6},{6,7},{7,4},{8,9},{9,10},{10,1... | collective-permute-start | bytes 3145736 | tf_op jit(solution)/shard_map/ppermute | solution.py:17
  27.6 34.4 %copy-start.5 = (s32[4,64]{1,0:T(4,128)S(1)}, s32[4,64]{1,0:T(4,128)}, u32[]{:S(2)}) copy-start(s32[4,64]{1,0:T(4,128)} %param.13) | copy-start | bytes 3076
  27.6 35.3 %copy-start.4 = (bf16[256,2048]{1,0:T(8,128)(2,1)S(1)}, bf16[256,2048]{1,0:T(8,128)(2,1)}, u32[]{:S(2)}) copy-start(bf16[256,2048]{1,0:T(8,128)(2,1)} %param.7) | copy-start | bytes 3145732
  52.6 90.5 %collective-permute-start.5 = (bf16[256,8192]{1,0:T(8,128)(2,1)}, bf16[256,8192]{1,0:T(8,128)(2,1)}, u32[]{:S(2)}, u32[]{:S(2)}) collective-permute-start(bf16[256,8192]{1,0:T(8,128)(2,1)} %constant_dynamic-update-slice_fusion), channel_id=1, source_target_pairs={{0,12},{4,16},{8,20},{12,24},{16,28},{20,32},{24,36},{28,40},{32,4... | collective-permute-start | bytes 12582920 | tf_op jit(solution)/shard_map/ppermute | solution.py:30
  54.5 190.4 %collective-permute-start.4 = (bf16[256,8192]{1,0:T(8,128)(2,1)}, bf16[256,8192]{1,0:T(8,128)(2,1)}, u32[]{:S(2)}, u32[]{:S(2)}) collective-permute-start(bf16[256,8192]{1,0:T(8,128)(2,1)} %constant_dynamic-update-slice_fusion), channel_id=1, source_target_pairs={{0,8},{4,12},{8,16},{12,20},{16,24},{20,28},{24,32},{28,36},{32,40... | collective-permute-start | bytes 12582920 | tf_op jit(solution)/shard_map/ppermute | solution.py:30
  58.0 233.9 %collective-permute-start.3 = (bf16[256,8192]{1,0:T(8,128)(2,1)}, bf16[256,8192]{1,0:T(8,128)(2,1)}, u32[]{:S(2)}, u32[]{:S(2)}) collective-permute-start(bf16[256,8192]{1,0:T(8,128)(2,1)} %constant_dynamic-update-slice_fusion), channel_id=1, source_target_pairs={{0,4},{4,8},{8,12},{12,16},{16,20},{20,24},{24,28},{28,32},{32,36}... | collective-permute-start | bytes 12582920 | tf_op jit(solution)/shard_map/ppermute | solution.py:30
  63.5 0.8 copy-start.7
  64.0 2.2 copy-start
  70.4 72.7 %copy-start.1 = (bf16[8192,256]{1,0:T(8,128)(2,1)S(1)}, bf16[8192,256]{1,0:T(8,128)(2,1)}, u32[]{:S(2)}) copy-start(bf16[8192,256]{1,0:T(8,128)(2,1)} %param.9) | copy-start | bytes 12582916
  250.3 47.0 %copy-start.6 = (f32[128]{0:T(128)S(1)}, f32[128]{0:T(128)}, u32[]{:S(2)}) copy-start(f32[128]{0:T(128)} %param.12) | copy-start | bytes 1540
  303.4 2.2 copy-start.2
